TPU v7x, 128 devices: a whole 4x4x4 slice. The times are simulated.
128 devices in a mesh: dp: 4 (over y), seq: 32 (over z, x, core).
Axes of the slice: x: 4, y: 4, z: 4, core: 2. Of those that a mesh axis runs over, the one named last changes fastest.
Arguments:
- queries: bfloat16 [4096, 8, 16, 128], P('seq', 'dp'), may hold values from -48 to 48
- keys_in: bfloat16 [4096, 8, 16, 128], P('seq', 'dp'), may hold values from -48 to 48
- values_in: bfloat16 [4096, 8, 16, 128], P('seq', 'dp'), may hold values from -6 to 6
- pair_keys: int32 [64, 27], replicated, may hold values from -1 to 63, as said below
- out_weight: bfloat16 [2048, 1536], P('seq', 'dp'), may hold values from -0.125 to 0.125
- cotangent: bfloat16 [4096, 8, 1536], P('seq', 'dp'), may hold values from -6 to 6
Outputs:
- output: bfloat16 [4096, 8, 1536], P('seq', 'dp')
- grad_queries: bfloat16 [4096, 8, 16, 128], P('seq', 'dp')
- grad_keys: bfloat16 [4096, 8, 16, 128], P('seq', 'dp')
- grad_values: bfloat16 [4096, 8, 16, 128], P('seq', 'dp')
- weight_grad: float32 [2048, 1536], P('seq', 'dp')
Inputs may be any that keep to these rules, and one draw needn't show every extreme that they name: `pair_keys`: A tile's row lists the tiles whose frame, row and column tile positions each differ from its own by at most one, itself included, in increasing order, then -1 in the remaining slots; the positions of the tiles in the 4 by 4 by 4 grid are a permutation drawn anew.
All inputs are finite; a program needn't handle non-finite values.
Results may differ from a plain program's by a relative error of at most 0.022.
Values may be sent and summed in bfloat16 or wider, within the bound.
No kernel may reach another device: no remote copies, remote signals or barrier semaphores. Data moves between devices by JAX's collectives and lax.ppermute only.
A program may use at most 320 MiB of HBM per device.

v0:
```python
import jax
import jax.numpy as jnp
from jax import lax
from jax.sharding import PartitionSpec as P


def tile_selector(key_index, tile_count):
    tile_ids = jnp.arange(tile_count, dtype=jnp.int32)
    return (key_index[:, :, None] == tile_ids[None, None, :]).astype(jnp.bfloat16)


def block_scores(query_block, key_block, key_index, score_scale):
    usable = key_index >= 0
    scores = (
        jnp.einsum("qad,qkbd->qakb", query_block, key_block, preferred_element_type=jnp.float32)
        * score_scale
    )
    return jnp.where(usable[:, None, :, None], scores, -jnp.inf)


def unit_forward(query_unit, key_unit, value_unit, pair_keys):
    tile_count, slot_count = pair_keys.shape
    tokens_all, head_size = query_unit.shape
    tile_len = tokens_all // tile_count
    score_scale = head_size ** (-0.5)
    both_tiles = jnp.concatenate(
        (
            key_unit.reshape(tile_count, tile_len, head_size),
            value_unit.reshape(tile_count, tile_len, head_size),
        ),
        axis=2,
    )
    query_blocks = query_unit.reshape(tile_count // 8, 8, tile_len, head_size)
    key_table = pair_keys.reshape(tile_count // 8, 8, slot_count)

    def one_block(packed):
        query_block, key_index = packed
        selector = tile_selector(key_index, tile_count)
        gathered = jnp.einsum(
            "qkt,tbd->qkbd", selector, both_tiles, preferred_element_type=jnp.float32
        ).astype(jnp.bfloat16)
        key_block = gathered[..., :head_size]
        value_block = gathered[..., head_size:]
        scores = block_scores(query_block, key_block, key_index, score_scale)
        row_max = jnp.max(scores, axis=(2, 3), keepdims=True)
        log_total = row_max + jnp.log(
            jnp.sum(jnp.exp(scores - row_max), axis=(2, 3), keepdims=True)
        )
        weights = jnp.exp(scores - log_total).astype(jnp.bfloat16)
        result = jnp.einsum(
            "qakb,qkbd->qad", weights, value_block, preferred_element_type=jnp.float32
        )
        return (result.astype(jnp.bfloat16), log_total[:, :, 0, 0], gathered)

    unit_outs, unit_sums, unit_gathered = lax.map(one_block, (query_blocks, key_table))
    return (unit_outs.reshape(tokens_all, head_size), unit_sums.reshape(tokens_all), unit_gathered)


def unit_backward(query_unit, gathered_unit, out_unit, log_unit, grad_unit, pair_keys):
    tile_count, slot_count = pair_keys.shape
    tokens_all, head_size = query_unit.shape
    tile_len = tokens_all // tile_count
    score_scale = head_size ** (-0.5)
    row_delta = jnp.sum(grad_unit.astype(jnp.float32) * out_unit.astype(jnp.float32), axis=-1)
    blocks = tile_count // 8
    packed = (
        query_unit.reshape(blocks, 8, tile_len, head_size),
        grad_unit.reshape(blocks, 8, tile_len, head_size),
        row_delta.reshape(blocks, 8, tile_len),
        log_unit.reshape(blocks, 8, tile_len),
        pair_keys.reshape(blocks, 8, slot_count),
        gathered_unit,
    )

    def one_block(carry, inputs):
        key_acc, value_acc = carry
        query_block, grad_block, delta_block, log_block, key_index, gathered = inputs
        selector = tile_selector(key_index, tile_count)
        key_block = gathered[..., :head_size]
        value_block = gathered[..., head_size:]
        scores = block_scores(query_block, key_block, key_index, score_scale)
        prob_full = jnp.exp(scores - log_block[:, :, None, None])
        weights = prob_full.astype(jnp.bfloat16)
        grad_probs = jnp.einsum(
            "qad,qkbd->qakb", grad_block, value_block, preferred_element_type=jnp.float32
        )
        grad_scores = (
            prob_full * (grad_probs - delta_block[:, :, None, None]) * score_scale
        ).astype(jnp.bfloat16)
        query_grad = jnp.einsum(
            "qakb,qkbd->qad", grad_scores, key_block, preferred_element_type=jnp.float32
        ).astype(jnp.bfloat16)
        weights_dense = jnp.einsum(
            "qakb,qkt->qatb", weights, selector, preferred_element_type=jnp.float32
        ).astype(jnp.bfloat16)
        scores_dense = jnp.einsum(
            "qakb,qkt->qatb", grad_scores, selector, preferred_element_type=jnp.float32
        ).astype(jnp.bfloat16)
        value_acc = value_acc + jnp.einsum(
            "qatb,qad->tbd", weights_dense, grad_block, preferred_element_type=jnp.float32
        )
        key_acc = key_acc + jnp.einsum(
            "qatb,qad->tbd", scores_dense, query_block, preferred_element_type=jnp.float32
        )
        return ((key_acc, value_acc), query_grad)

    empty_acc = jnp.zeros((tile_count, tile_len, head_size), jnp.float32)
    (key_acc, value_acc), query_grads = lax.scan(one_block, (empty_acc, empty_acc), packed)
    return (
        query_grads.reshape(tokens_all, head_size),
        key_acc.reshape(tokens_all, head_size).astype(jnp.bfloat16),
        value_acc.reshape(tokens_all, head_size).astype(jnp.bfloat16),
    )


def local(queries, keys_in, values_in, pair_keys, out_weight, cotangent):
    tok_rows, local_videos, head_count, head_size = queries.shape
    unit_total = local_videos * head_count
    seq_size = lax.axis_size("seq")
    units_here = unit_total // seq_size
    row_count = tok_rows * local_videos
    width_heads = head_count * head_size
    split_shape = (tok_rows, seq_size, units_here, head_size)
    query_all = lax.all_to_all(
        queries.reshape(split_shape), "seq", split_axis=1, concat_axis=0, tiled=True
    )
    key_all = lax.all_to_all(
        keys_in.reshape(split_shape), "seq", split_axis=1, concat_axis=0, tiled=True
    )
    value_all = lax.all_to_all(
        values_in.reshape(split_shape), "seq", split_axis=1, concat_axis=0, tiled=True
    )
    item_index = 0
    result, log_total, gathered = unit_forward(
        query_all[:, 0, item_index],
        key_all[:, 0, item_index],
        value_all[:, 0, item_index],
        pair_keys,
    )
    unit_outs = [result]
    unit_sums = [log_total]
    unit_gathered = [gathered]
    heads_out = jnp.stack(unit_outs, 1)[:, None]
    heads_log = jnp.stack(unit_sums, 1)[:, None]
    heads_gathered = jnp.stack(unit_gathered, 2)
    attn_tok = lax.all_to_all(heads_out, "seq", split_axis=0, concat_axis=1, tiled=True)
    attn_rows = attn_tok.reshape(row_count, width_heads)
    cot_rows = cotangent.reshape(row_count, cotangent.shape[2])
    weight_cols = lax.all_gather(out_weight, "dp", axis=1, tiled=True)
    weight_full = lax.all_gather(weight_cols, "seq", axis=0, tiled=True)
    projected = jnp.dot(attn_rows, weight_full, preferred_element_type=jnp.float32)
    grad_attention = jnp.einsum(
        "rd,cd->rc", cot_rows, weight_full, preferred_element_type=jnp.float32
    ).astype(jnp.bfloat16)
    output = projected.astype(jnp.bfloat16).reshape(tok_rows, local_videos, cotangent.shape[2])
    by_rows = lax.psum_scatter(
        jnp.einsum("rc,rd->cd", attn_rows, cot_rows, preferred_element_type=jnp.float32).astype(
            jnp.bfloat16
        ),
        "seq",
        scatter_dimension=0,
        tiled=True,
    )
    weight_grad = lax.psum_scatter(by_rows, "dp", scatter_dimension=1, tiled=True).astype(
        jnp.float32
    )
    grad_heads = lax.all_to_all(
        grad_attention.reshape(split_shape), "seq", split_axis=1, concat_axis=0, tiled=True
    )
    item_index = 0
    grad_q, grad_k, grad_v = unit_backward(
        query_all[:, 0, item_index],
        heads_gathered[:, :, item_index],
        heads_out[:, 0, item_index],
        heads_log[:, 0, item_index],
        grad_heads[:, 0, item_index],
        pair_keys,
    )
    query_parts = [grad_q]
    key_parts = [grad_k]
    value_parts = [grad_v]
    grad_query_tok, grad_key_tok, grad_value_tok = (
        lax.all_to_all(
            jnp.stack(query_parts, 1)[:, None], "seq", split_axis=0, concat_axis=1, tiled=True
        ),
        lax.all_to_all(
            jnp.stack(key_parts, 1)[:, None], "seq", split_axis=0, concat_axis=1, tiled=True
        ),
        lax.all_to_all(
            jnp.stack(value_parts, 1)[:, None], "seq", split_axis=0, concat_axis=1, tiled=True
        ),
    )
    full_shape = (tok_rows, local_videos, head_count, head_size)
    return (
        output,
        grad_query_tok.reshape(full_shape),
        grad_key_tok.reshape(full_shape),
        grad_value_tok.reshape(full_shape),
        weight_grad,
    )


def solution(mesh):
    placed = (
        P("seq", "dp", None, None),
        P("seq", "dp", None, None),
        P("seq", "dp", None, None),
        P(),
        P("seq", "dp"),
        P("seq", "dp", None),
    )
    return jax.shard_map(
        local,
        mesh=mesh,
        in_specs=placed,
        out_specs=(
            P("seq", "dp", None),
            P("seq", "dp", None, None),
            P("seq", "dp", None, None),
            P("seq", "dp", None, None),
            P("seq", "dp"),
        ),
        check_vma=False,
    )
```

profile of v0, /device:TPU:0, one launch (start us, length us, event | category | flops | bytes accessed | tf_op | source)
XLA Modules:
  0.0 910.3 jit_solution(14114918590238716047)
XLA Ops:
  20.7 14.7 %all-to-all-done.1 = bf16[128,32,1,128]{3,0,2,1:T(8,128)(2,1)S(1)} async-done(((bf16[128,32,1,128]{3,0,2,1:T(8,128)(2,1)}), bf16[128,32,1,128]{3,0,2,1:T(8,128)(2,1)S(1)}, u32[]{:S(2)}, u32[]{:S(2)}) %all-to-all-start.1) | async-done | bytes 1048608 | tf_op jit(solution)/shard_map/all_to_all | solution.py:127
  40.8 15.9 %all-to-all-done.2 = bf16[128,32,1,128]{3,0,2,1:T(8,128)(2,1)S(1)} async-done(((bf16[128,32,1,128]{3,0,2,1:T(8,128)(2,1)}), bf16[128,32,1,128]{3,0,2,1:T(8,128)(2,1)S(1)}, u32[]{:S(2)}, u32[]{:S(2)}) %all-to-all-start.2) | async-done | bytes 1048608 | tf_op jit(solution)/shard_map/all_to_all | solution.py:130
  61.5 13.5 %all_gather.6 = bf16[64,1536]{1,0:T(8,128)(2,1)} all-gather(bf16[64,384]{1,0:T(8,128)(2,1)S(1)} %copy-done.15), channel_id=1, replica_groups=mesh['dp'=4,'seq'=32] {'dp'}, dimensions={1}, use_global_device_ids=true | all-gather | bytes 245760 | tf_op jit(solution)/shard_map/all_gather | solution.py:149
  79.9 177.9 %while.29 = (s32[]{:T(128)}, bf16[8,8,64,128]{3,2,1,0:T(8,128)(2,1)}, f32[8,8,64]{2,1,0:T(8,128)}, bf16[8,8,27,64,256]{4,3,2,1,0:T(8,128)(2,1)}, s32[8,8,27]{2,1...) while((s32[]{:T(128)}, ...), condition=%wide.region_3.4_spmd, body=%wide.region_0.3_spmd.sunk | while | flops 919319808 | bytes 55467480 | solution.py:55
  310.3 491.1 %while.30 = (s32[]{:T(128)}, f32[64,64,128]{2,1,0:T(8,128)}, f32[64,64,128]{2,1,0:T(8,128)}, bf16[8,8,64,128]{3,2,1,0:T(8,128)(2,1)}, s32[8,8,27]{2,1,0:T(8,128)...) while((s32[]{:T(128)}, f32[64,64,128]{2,1,0:T(8,128)}, ...), condition=%wide.region_6.7_spmd.clone, body=%wide.region_5.6_spmd.clone.sunk | while | flops 1995828480 | bytes 147016176 | solution.py:108
  354.7 16.5 %bitcast_add_fusion.4 = f32[64,64,128]{2,1,0:T(8,128)} fusion(f32[64,64,128]{2,1,0:T(8,128)} %get-tuple-element.452, bf16[8,64,64,64]{3,2,1,0:T(8,128)(2,1)} %convert_bitcast_fusion.4, pred[]{:T(512)S(6)} %compare.3, bf16[8,8,64,128]{3,2,1,0:T(8,128)(2,1)} %get-tuple-element.468, s32[]{:T(128)} %get-tuple-element.451), kind=kOutput, calls=%fused_computation.50.clone.1 | convolution fusion | flops 537919488 | bytes 12714497 | tf_op jit(solution)/shard_map/while/body/eval_jaxpr/qatb,qad->tbd/dot_general | solution.py:102
  375.9 13.9 %bitcast_add_fusion.5 = f32[64,64,128]{2,1,0:T(8,128)} fusion(f32[64,64,128]{2,1,0:T(8,128)} %get-tuple-element.453, bf16[8,64,64,64]{3,2,1,0:T(8,128)(2,1)S(1)} %convert_bitcast_fusion.5, pred[]{:T(512)S(6)} %compare.3, bf16[8,8,64,128]{3,2,1,0:T(8,128)(2,1)} %get-tuple-element.471, s32[]{:T(128)} %get-tuple-element.451), kind=kOutput, calls=%fused_computation.49.clone.1 | convolution fusion | flops 537919488 | bytes 8520193 | tf_op jit(solution)/shard_map/while/body/eval_jaxpr/qatb,qad->tbd/dot_general | solution.py:99
  411.2 17.0 %bitcast_add_fusion.4 = f32[64,64,128]{2,1,0:T(8,128)} fusion(f32[64,64,128]{2,1,0:T(8,128)} %get-tuple-element.452, bf16[8,64,64,64]{3,2,1,0:T(8,128)(2,1)} %convert_bitcast_fusion.4, pred[]{:T(512)S(6)} %compare.3, bf16[8,8,64,128]{3,2,1,0:T(8,128)(2,1)} %get-tuple-element.468, s32[]{:T(128)} %get-tuple-element.451), kind=kOutput, calls=%fused_computation.50.clone.1 | convolution fusion | flops 537919488 | bytes 12714497 | tf_op jit(solution)/shard_map/while/body/eval_jaxpr/qatb,qad->tbd/dot_general | solution.py:102
  433.0 14.7 %bitcast_add_fusion.5 = f32[64,64,128]{2,1,0:T(8,128)} fusion(f32[64,64,128]{2,1,0:T(8,128)} %get-tuple-element.453, bf16[8,64,64,64]{3,2,1,0:T(8,128)(2,1)S(1)} %convert_bitcast_fusion.5, pred[]{:T(512)S(6)} %compare.3, bf16[8,8,64,128]{3,2,1,0:T(8,128)(2,1)} %get-tuple-element.471, s32[]{:T(128)} %get-tuple-element.451), kind=kOutput, calls=%fused_computation.49.clone.1 | convolution fusion | flops 537919488 | bytes 8520193 | tf_op jit(solution)/shard_map/while/body/eval_jaxpr/qatb,qad->tbd/dot_general | solution.py:99
  469.0 17.0 %bitcast_add_fusion.4 = f32[64,64,128]{2,1,0:T(8,128)} fusion(f32[64,64,128]{2,1,0:T(8,128)} %get-tuple-element.452, bf16[8,64,64,64]{3,2,1,0:T(8,128)(2,1)} %convert_bitcast_fusion.4, pred[]{:T(512)S(6)} %compare.3, bf16[8,8,64,128]{3,2,1,0:T(8,128)(2,1)} %get-tuple-element.468, s32[]{:T(128)} %get-tuple-element.451), kind=kOutput, calls=%fused_computation.50.clone.1 | convolution fusion | flops 537919488 | bytes 12714497 | tf_op jit(solution)/shard_map/while/body/eval_jaxpr/qatb,qad->tbd/dot_general | solution.py:102
  490.8 14.7 %bitcast_add_fusion.5 = f32[64,64,128]{2,1,0:T(8,128)} fusion(f32[64,64,128]{2,1,0:T(8,128)} %get-tuple-element.453, bf16[8,64,64,64]{3,2,1,0:T(8,128)(2,1)S(1)} %convert_bitcast_fusion.5, pred[]{:T(512)S(6)} %compare.3, bf16[8,8,64,128]{3,2,1,0:T(8,128)(2,1)} %get-tuple-element.471, s32[]{:T(128)} %get-tuple-element.451), kind=kOutput, calls=%fused_computation.49.clone.1 | convolution fusion | flops 537919488 | bytes 8520193 | tf_op jit(solution)/shard_map/while/body/eval_jaxpr/qatb,qad->tbd/dot_general | solution.py:99
  526.9 17.0 %bitcast_add_fusion.4 = f32[64,64,128]{2,1,0:T(8,128)} fusion(f32[64,64,128]{2,1,0:T(8,128)} %get-tuple-element.452, bf16[8,64,64,64]{3,2,1,0:T(8,128)(2,1)} %convert_bitcast_fusion.4, pred[]{:T(512)S(6)} %compare.3, bf16[8,8,64,128]{3,2,1,0:T(8,128)(2,1)} %get-tuple-element.468, s32[]{:T(128)} %get-tuple-element.451), kind=kOutput, calls=%fused_computation.50.clone.1 | convolution fusion | flops 537919488 | bytes 12714497 | tf_op jit(solution)/shard_map/while/body/eval_jaxpr/qatb,qad->tbd/dot_general | solution.py:102
  548.6 14.7 %bitcast_add_fusion.5 = f32[64,64,128]{2,1,0:T(8,128)} fusion(f32[64,64,128]{2,1,0:T(8,128)} %get-tuple-element.453, bf16[8,64,64,64]{3,2,1,0:T(8,128)(2,1)S(1)} %convert_bitcast_fusion.5, pred[]{:T(512)S(6)} %compare.3, bf16[8,8,64,128]{3,2,1,0:T(8,128)(2,1)} %get-tuple-element.471, s32[]{:T(128)} %get-tuple-element.451), kind=kOutput, calls=%fused_computation.49.clone.1 | convolution fusion | flops 537919488 | bytes 8520193 | tf_op jit(solution)/shard_map/while/body/eval_jaxpr/qatb,qad->tbd/dot_general | solution.py:99
  584.7 17.0 %bitcast_add_fusion.4 = f32[64,64,128]{2,1,0:T(8,128)} fusion(f32[64,64,128]{2,1,0:T(8,128)} %get-tuple-element.452, bf16[8,64,64,64]{3,2,1,0:T(8,128)(2,1)} %convert_bitcast_fusion.4, pred[]{:T(512)S(6)} %compare.3, bf16[8,8,64,128]{3,2,1,0:T(8,128)(2,1)} %get-tuple-element.468, s32[]{:T(128)} %get-tuple-element.451), kind=kOutput, calls=%fused_computation.50.clone.1 | convolution fusion | flops 537919488 | bytes 12714497 | tf_op jit(solution)/shard_map/while/body/eval_jaxpr/qatb,qad->tbd/dot_general | solution.py:102
  606.4 14.7 %bitcast_add_fusion.5 = f32[64,64,128]{2,1,0:T(8,128)} fusion(f32[64,64,128]{2,1,0:T(8,128)} %get-tuple-element.453, bf16[8,64,64,64]{3,2,1,0:T(8,128)(2,1)S(1)} %convert_bitcast_fusion.5, pred[]{:T(512)S(6)} %compare.3, bf16[8,8,64,128]{3,2,1,0:T(8,128)(2,1)} %get-tuple-element.471, s32[]{:T(128)} %get-tuple-element.451), kind=kOutput, calls=%fused_computation.49.clone.1 | convolution fusion | flops 537919488 | bytes 8520193 | tf_op jit(solution)/shard_map/while/body/eval_jaxpr/qatb,qad->tbd/dot_general | solution.py:99
  642.5 17.0 %bitcast_add_fusion.4 = f32[64,64,128]{2,1,0:T(8,128)} fusion(f32[64,64,128]{2,1,0:T(8,128)} %get-tuple-element.452, bf16[8,64,64,64]{3,2,1,0:T(8,128)(2,1)} %convert_bitcast_fusion.4, pred[]{:T(512)S(6)} %compare.3, bf16[8,8,64,128]{3,2,1,0:T(8,128)(2,1)} %get-tuple-element.468, s32[]{:T(128)} %get-tuple-element.451), kind=kOutput, calls=%fused_computation.50.clone.1 | convolution fusion | flops 537919488 | bytes 12714497 | tf_op jit(solution)/shard_map/while/body/eval_jaxpr/qatb,qad->tbd/dot_general | solution.py:102
  664.2 14.7 %bitcast_add_fusion.5 = f32[64,64,128]{2,1,0:T(8,128)} fusion(f32[64,64,128]{2,1,0:T(8,128)} %get-tuple-element.453, bf16[8,64,64,64]{3,2,1,0:T(8,128)(2,1)S(1)} %convert_bitcast_fusion.5, pred[]{:T(512)S(6)} %compare.3, bf16[8,8,64,128]{3,2,1,0:T(8,128)(2,1)} %get-tuple-element.471, s32[]{:T(128)} %get-tuple-element.451), kind=kOutput, calls=%fused_computation.49.clone.1 | convolution fusion | flops 537919488 | bytes 8520193 | tf_op jit(solution)/shard_map/while/body/eval_jaxpr/qatb,qad->tbd/dot_general | solution.py:99
  700.3 17.0 %bitcast_add_fusion.4 = f32[64,64,128]{2,1,0:T(8,128)} fusion(f32[64,64,128]{2,1,0:T(8,128)} %get-tuple-element.452, bf16[8,64,64,64]{3,2,1,0:T(8,128)(2,1)} %convert_bitcast_fusion.4, pred[]{:T(512)S(6)} %compare.3, bf16[8,8,64,128]{3,2,1,0:T(8,128)(2,1)} %get-tuple-element.468, s32[]{:T(128)} %get-tuple-element.451), kind=kOutput, calls=%fused_computation.50.clone.1 | convolution fusion | flops 537919488 | bytes 12714497 | tf_op jit(solution)/shard_map/while/body/eval_jaxpr/qatb,qad->tbd/dot_general | solution.py:102
  722.1 14.7 %bitcast_add_fusion.5 = f32[64,64,128]{2,1,0:T(8,128)} fusion(f32[64,64,128]{2,1,0:T(8,128)} %get-tuple-element.453, bf16[8,64,64,64]{3,2,1,0:T(8,128)(2,1)S(1)} %convert_bitcast_fusion.5, pred[]{:T(512)S(6)} %compare.3, bf16[8,8,64,128]{3,2,1,0:T(8,128)(2,1)} %get-tuple-element.471, s32[]{:T(128)} %get-tuple-element.451), kind=kOutput, calls=%fused_computation.49.clone.1 | convolution fusion | flops 537919488 | bytes 8520193 | tf_op jit(solution)/shard_map/while/body/eval_jaxpr/qatb,qad->tbd/dot_general | solution.py:99
  758.1 17.0 %bitcast_add_fusion.4 = f32[64,64,128]{2,1,0:T(8,128)} fusion(f32[64,64,128]{2,1,0:T(8,128)} %get-tuple-element.452, bf16[8,64,64,64]{3,2,1,0:T(8,128)(2,1)} %convert_bitcast_fusion.4, pred[]{:T(512)S(6)} %compare.3, bf16[8,8,64,128]{3,2,1,0:T(8,128)(2,1)} %get-tuple-element.468, s32[]{:T(128)} %get-tuple-element.451), kind=kOutput, calls=%fused_computation.50.clone.1 | convolution fusion | flops 537919488 | bytes 12714497 | tf_op jit(solution)/shard_map/while/body/eval_jaxpr/qatb,qad->tbd/dot_general | solution.py:102
  779.9 14.7 %bitcast_add_fusion.5 = f32[64,64,128]{2,1,0:T(8,128)} fusion(f32[64,64,128]{2,1,0:T(8,128)} %get-tuple-element.453, bf16[8,64,64,64]{3,2,1,0:T(8,128)(2,1)S(1)} %convert_bitcast_fusion.5, pred[]{:T(512)S(6)} %compare.3, bf16[8,8,64,128]{3,2,1,0:T(8,128)(2,1)} %get-tuple-element.471, s32[]{:T(128)} %get-tuple-element.451), kind=kOutput, calls=%fused_computation.49.clone.1 | convolution fusion | flops 537919488 | bytes 8520193 | tf_op jit(solution)/shard_map/while/body/eval_jaxpr/qatb,qad->tbd/dot_general | solution.py:99
  814.0 13.0 %all-to-all-done.6 = bf16[32,2,8192]{2,1,0:T(2,128)(2,1)S(1)} async-done(((bf16[32,2,8192]{2,1,0:T(2,128)(2,1)}), bf16[32,2,8192]{2,1,0:T(2,128)(2,1)S(1)}, u32[]{:S(2)}, u32[]{:S(2)}) %all-to-all-start.6) | async-done | bytes 1048608 | tf_op jit(solution)/shard_map/all_to_all | solution.py:186
  836.4 11.9 %all-to-all-done.7 = bf16[32,2,8192]{2,1,0:T(2,128)(2,1)S(1)} async-done(((bf16[32,2,8192]{2,1,0:T(2,128)(2,1)}), bf16[32,2,8192]{2,1,0:T(2,128)(2,1)S(1)}, u32[]{:S(2)}, u32[]{:S(2)}) %all-to-all-start.7) | async-done | bytes 1048608 | tf_op jit(solution)/shard_map/all_to_all | solution.py:189
  854.9 23.6 %reduce-scatter.7.cloned.1.call-done = bf16[384,64]{1,0:T(8,128)(2,1)} async-done(((bf16[1536,64]{1,0:T(8,128)(2,1)}), bf16[384,64]{1,0:T(8,128)(2,1)}) %reduce-scatter.7.cloned.1.call-update) | async-done | bytes 49168
  (342 shorter events, 519.2 us)
Async XLA Ops:
  7.2 32.2 %copy-start.9 = (bf16[128,2,16,128]{3,2,1,0:T(8,128)(2,1)S(1)}, bf16[128,2,16,128]{3,2,1,0:T(8,128)(2,1)}, u32[]{:S(2)}) copy-start(bf16[128,2,16,128]{3,2,1,0:T(8,128)(2,1)} %param.10) | copy-start | bytes 3145732
  7.2 54.3 %copy-start.15 = (bf16[64,384]{1,0:T(8,128)(2,1)S(1)}, bf16[64,384]{1,0:T(8,128)(2,1)}, u32[]{:S(2)}) copy-start(bf16[64,384]{1,0:T(8,128)(2,1)} %param.14) | copy-start | bytes 147460
  7.2 67.8 %copy-start.16 = (s32[64,27]{0,1:T(8,128)S(1)}, s32[64,27]{0,1:T(8,128)}, u32[]{:S(2)}) copy-start(s32[64,27]{0,1:T(8,128)} %param.13) | copy-start | bytes 20740
  9.9 25.6 %all-to-all-start.1 = ((bf16[128,32,1,128]{3,0,2,1:T(8,128)(2,1)}), bf16[128,32,1,128]{3,0,2,1:T(8,128)(2,1)S(1)}, u32[]{:S(2)}, u32[]{:S(2)}) async-start(bf16[128,32,1,128]{3,0,2,1:T(8,128)(2,1)} %bitcast.17), calls=%async_computation.1 | async-start | bytes 2097152 | tf_op jit(solution)/shard_map/all_to_all | solution.py:127
  35.5 21.3 %all-to-all-start.2 = ((bf16[128,32,1,128]{3,0,2,1:T(8,128)(2,1)}), bf16[128,32,1,128]{3,0,2,1:T(8,128)(2,1)S(1)}, u32[]{:S(2)}, u32[]{:S(2)}) async-start(bf16[128,32,1,128]{3,0,2,1:T(8,128)(2,1)} %bitcast.21), calls=%async_computation.2 | async-start | bytes 2097152 | tf_op jit(solution)/shard_map/all_to_all | solution.py:130
  56.7 22.0 %all-to-all-start = ((bf16[128,32,1,128]{3,0,2,1:T(8,128)(2,1)}), bf16[128,32,1,128]{3,0,2,1:T(8,128)(2,1)}, u32[]{:S(2)}, u32[]{:S(2)}) async-start(bf16[128,32,1,128]{3,0,2,1:T(8,128)(2,1)} %bitcast.13), calls=%async_computation | async-start | bytes 2097152 | tf_op jit(solution)/shard_map/all_to_all | solution.py:124
  61.4 206.4 %all-gather.2.cloned.1.call-start = ((), (), s32[]{:S(2)}) async-start(), calls=%async_computation.10 | async-start | bytes 6488064 | tf_op jit(solution)/shard_map/all_gather | solution.py:150
  262.2 22.6 %all-to-all-start.3 = ((bf16[32,2,8192]{2,1,0:T(2,128)(2,1)}), bf16[32,2,8192]{2,1,0:T(2,128)(2,1)S(1)}, u32[]{:S(2)}, u32[]{:S(2)}) async-start(bf16[32,2,8192]{2,1,0:T(2,128)(2,1)} %reshape.163), calls=%async_computation.3 | async-start | bytes 2097152 | tf_op jit(solution)/shard_map/all_to_all | solution.py:146
  284.8 22.0 %all-to-all-start.4 = ((bf16[128,32,1,128]{3,0,2,1:T(8,128)(2,1)}), bf16[128,32,1,128]{3,0,2,1:T(8,128)(2,1)}, u32[]{:S(2)}, u32[]{:S(2)}) async-start(bf16[128,32,1,128]{3,0,2,1:T(8,128)(2,1)} %copy.85), calls=%async_computation.4 | async-start | bytes 2097152 | tf_op jit(solution)/shard_map/all_to_all | solution.py:167
  289.4 563.6 %reduce-scatter.5.cloned.1.call-start = ((), (), s32[]{:S(2)}) async-start(), calls=%async_computation.11 | async-start | bytes 6488064 | tf_op jit(solution)/shard_map/reduce_scatter | solution.py:156
  411.2 17.0 %copy-start.3 = (bf16[8,64,27,64]{3,1,2,0:T(8,128)(2,1)S(1)}, bf16[8,64,27,64]{3,1,2,0:T(8,128)(2,1)}, u32[]{:S(2)}) copy-start(bf16[8,64,27,64]{3,1,2,0:T(8,128)(2,1)} %copy-done.2) | copy-start | bytes 5308420 | tf_op jit(solution)/shard_map/while
  469.0 17.0 %copy-start.1 = (bf16[8,27,64,256]{3,2,1,0:T(8,128)(2,1)S(1)}, bf16[8,27,64,256]{3,2,1,0:T(8,128)(2,1)}, u32[]{:S(2)}) copy-start(bf16[8,27,64,256]{3,2,1,0:T(8,128)(2,1)} %copy-done) | copy-start | bytes 21233668 | tf_op jit(solution)/shard_map/while
  469.0 17.0 %copy-start.3 = (bf16[8,64,27,64]{3,1,2,0:T(8,128)(2,1)S(1)}, bf16[8,64,27,64]{3,1,2,0:T(8,128)(2,1)}, u32[]{:S(2)}) copy-start(bf16[8,64,27,64]{3,1,2,0:T(8,128)(2,1)} %copy-done.2) | copy-start | bytes 5308420 | tf_op jit(solution)/shard_map/while
  526.9 17.0 %copy-start.3 = (bf16[8,64,27,64]{3,1,2,0:T(8,128)(2,1)S(1)}, bf16[8,64,27,64]{3,1,2,0:T(8,128)(2,1)}, u32[]{:S(2)}) copy-start(bf16[8,64,27,64]{3,1,2,0:T(8,128)(2,1)} %copy-done.2) | copy-start | bytes 5308420 | tf_op jit(solution)/shard_map/while
  584.7 17.0 %copy-start.3 = (bf16[8,64,27,64]{3,1,2,0:T(8,128)(2,1)S(1)}, bf16[8,64,27,64]{3,1,2,0:T(8,128)(2,1)}, u32[]{:S(2)}) copy-start(bf16[8,64,27,64]{3,1,2,0:T(8,128)(2,1)} %copy-done.2) | copy-start | bytes 5308420 | tf_op jit(solution)/shard_map/while
  642.5 17.0 %copy-start.3 = (bf16[8,64,27,64]{3,1,2,0:T(8,128)(2,1)S(1)}, bf16[8,64,27,64]{3,1,2,0:T(8,128)(2,1)}, u32[]{:S(2)}) copy-start(bf16[8,64,27,64]{3,1,2,0:T(8,128)(2,1)} %copy-done.2) | copy-start | bytes 5308420 | tf_op jit(solution)/shard_map/while
  700.3 17.0 %copy-start.3 = (bf16[8,64,27,64]{3,1,2,0:T(8,128)(2,1)S(1)}, bf16[8,64,27,64]{3,1,2,0:T(8,128)(2,1)}, u32[]{:S(2)}) copy-start(bf16[8,64,27,64]{3,1,2,0:T(8,128)(2,1)} %copy-done.2) | copy-start | bytes 5308420 | tf_op jit(solution)/shard_map/while
  758.1 17.0 %copy-start.3 = (bf16[8,64,27,64]{3,1,2,0:T(8,128)(2,1)S(1)}, bf16[8,64,27,64]{3,1,2,0:T(8,128)(2,1)}, u32[]{:S(2)}) copy-start(bf16[8,64,27,64]{3,1,2,0:T(8,128)(2,1)} %copy-done.2) | copy-start | bytes 5308420 | tf_op jit(solution)/shard_map/while
  805.8 21.3 %all-to-all-start.6 = ((bf16[32,2,8192]{2,1,0:T(2,128)(2,1)}), bf16[32,2,8192]{2,1,0:T(2,128)(2,1)S(1)}, u32[]{:S(2)}, u32[]{:S(2)}) async-start(bf16[32,2,8192]{2,1,0:T(2,128)(2,1)} %reshape.167), calls=%async_computation.6 | async-start | bytes 2097152 | tf_op jit(solution)/shard_map/all_to_all | solution.py:186
  812.9 67.3 %copy-start.5 = (bf16[256,2048]{1,0:T(8,128)(2,1)S(1)}, bf16[256,2048]{1,0:T(8,128)(2,1)}, u32[]{:S(2)}) copy-start(bf16[256,2048]{1,0:T(8,128)(2,1)} %copy-done.4) | copy-start | bytes 3145732
  827.0 21.3 %all-to-all-start.7 = ((bf16[32,2,8192]{2,1,0:T(2,128)(2,1)}), bf16[32,2,8192]{2,1,0:T(2,128)(2,1)S(1)}, u32[]{:S(2)}, u32[]{:S(2)}) async-start(bf16[32,2,8192]{2,1,0:T(2,128)(2,1)} %reshape.169), calls=%async_computation.7 | async-start | bytes 2097152 | tf_op jit(solution)/shard_map/all_to_all | solution.py:189
  848.3 37.4 %copy-start.6 = (bf16[32,2,8192]{2,1,0:T(2,128)(2,1)}, bf16[32,2,8192]{2,1,0:T(2,128)(2,1)S(1)}, u32[]{:S(2)}) copy-start(bf16[32,2,8192]{2,1,0:T(2,128)(2,1)S(1)} %all-to-all-done.7) | copy-start | bytes 3145732
  848.3 49.1 %all-to-all-start.5 = ((bf16[32,2,8192]{2,1,0:T(2,128)(2,1)}), bf16[32,2,8192]{2,1,0:T(2,128)(2,1)}, u32[]{:S(2)}, u32[]{:S(2)}) async-start(bf16[32,2,8192]{2,1,0:T(2,128)(2,1)} %reshape.165), calls=%async_computation.5 | async-start | bytes 2097152 | tf_op jit(solution)/shard_map/all_to_all | solution.py:183
  853.0 25.6 %reduce-scatter.7.cloned.1.call-start = ((), (), s32[]{:S(2)}) async-start(), calls=%async_computation.12 | async-start | bytes 491520
  (60 other events, 505.8 us)
Sparse Core Ops, SparseCore 0:
  75.1 50.0 all-gather.1
  296.6 87.0 reduce-scatter.4
  856.9 21.6 reduce-scatter.6
where the time goes:
time: 918 us; the launch traced here: 910 us
  matrix products  505 us (55%)
  local copies, waits for them, and re-layouts  169 us (18%)
  waiting for transfers between devices  101 us (11%)
  starting transfers between devices  39.4 us (4%)
  other arithmetic  36.2 us (4%)
  loops' own time  31.7 us (3%)
  between operations  14.3 us (2%)
  blocking collectives  13.5 us (1%)
    dot_general x8, matrix products, one_block(): jnp.einsum('qatb,qad->tbd', scores_dense, query_block, preferred_element_...  136 us
    dot_general x8, matrix products, one_block(): jnp.einsum('qatb,qad->tbd', weights_dense, grad_block, preferred_element_...  117 us
    dot_general x16, matrix products, block_scores(): jnp.einsum('qad,qkbd->qakb', query_block, key_block, preferred_element_ty...  65.7 us
    dynamic_update_slice x8, local copies, waits for them, and re-layouts, unit_forward(): lax.map(one_block, (query_blocks, key_table))  59.7 us
    dot_general x8, matrix products, one_block(): jnp.einsum('qakb,qkt->qatb', grad_scores, selector, preferred_element_typ...  51.9 us
    dot_general x8, matrix products, one_block(): jnp.einsum('qad,qkbd->qakb', grad_block, value_block, preferred_element_t...  34.1 us
    unnamed x39, local copies, waits for them, and re-layouts  32.1 us
    another operation x1, loops' own time, unit_backward(): lax.scan(one_block, (empty_acc, empty_acc), packed)  30.7 us
  transfers between devices with their start and end apart: 11, of which 8 were waited for; matrix products, arithmetic and copies ran while one was open for 75% of the time, Pallas kernels for 0%

commit v1 on v0

v1 whole, which is shorter than its diff:
```python
import functools

import jax
import jax.numpy as jnp
from jax import lax
from jax.experimental import pallas as pl
from jax.experimental.pallas import tpu as pltpu
from jax.sharding import PartitionSpec as P

F32, BF16 = jnp.float32, jnp.bfloat16
TILE = 64
SIDE = 4
ROW = SIDE * TILE
LOG2E = 1.4426950408889634
VMEM_BYTES = 60 * 1024 * 1024
NT = (((1,), (1,)), ((), ()))
NN = (((1,), (0,)), ((), ()))


def dot(a, b, dims=NN):
    return lax.dot_general(a, b, dims, preferred_element_type=F32)


def order_kernel(pairs_ref, order_ref):
    pairs = pairs_ref[...]
    tiles, slots = pairs.shape
    lane = lax.broadcasted_iota(jnp.int32, (tiles, tiles), 1)
    line = lax.broadcasted_iota(jnp.int32, (tiles, tiles), 0)
    near = jnp.zeros((tiles, tiles), F32)
    for slot in range(slots):
        near += (pairs[:, slot : slot + 1] == lane).astype(F32)
    near_b = near.astype(BF16)
    walks = dot(dot(near_b, near_b).astype(BF16), near_b)
    corner = jnp.sum(near, axis=0, keepdims=True) == 8.0
    ids = lane[:1]

    def first(mask):
        return jnp.min(jnp.where(mask, ids, tiles), axis=1, keepdims=True)

    def walks_from(tile):
        return jnp.sum(jnp.where(line == tile, walks, 0.0), axis=0, keepdims=True)

    base = walks_from(first(corner))
    ends = corner & (base == 16.0)
    place = jnp.zeros((1, tiles), jnp.int32)
    for _ in range(3):
        end = first(ends)
        ends = ends & (ids != end)
        far = walks_from(end)
        step = (
            (5.0 * far >= 3.0 * base).astype(jnp.int32)
            + (3.0 * far >= 5.0 * base).astype(jnp.int32)
            + (far >= 4.0 * base).astype(jnp.int32)
        )
        place = SIDE * place + step
    order_ref[...] = jnp.sum(jnp.where(place == line, lane, 0), axis=1, keepdims=True)


def grid_order(pair_keys):
    tiles = pair_keys.shape[0]
    return pl.pallas_call(
        order_kernel, out_shape=jax.ShapeDtypeStruct((tiles, 1), jnp.int32), name="grid_order"
    )(pair_keys).reshape(tiles)


def move_tiles(order_ref, remote, arrays, sem, inbound):
    @pl.loop(0, order_ref.shape[0])
    def _(place):
        tile = order_ref[place]
        far = remote.at[tile // 2, :, pl.ds(pl.multiple_of((tile % 2) * TILE, TILE), TILE)]
        here = arrays.at[:, pl.ds(pl.multiple_of(place * TILE, TILE), TILE)]
        if inbound:
            pltpu.make_async_copy(far, here, sem).start()
        else:
            pltpu.make_async_copy(here, far, sem).start()


def await_tiles(arrays, sem):
    pltpu.make_async_copy(arrays, arrays, sem).wait()


def transposed(source, target):
    for block in range(source.shape[0] // ROW):
        rows = pl.ds(block * ROW, ROW)
        target[:, rows] = source[rows, :].T


def window(r):
    low, high = max(r - 1, 0), min(r + 1, SIDE - 1)
    return low, high - low + 1


STARTS = [sum(window(i)[1] for i in range(r)) for r in range(SIDE + 1)]
LEFT = (slice(0, 3 * TILE), slice(0, 2 * TILE))
RIGHT = (slice(TILE, 4 * TILE), slice(2 * TILE, 4 * TILE))


def masked(scores, b):
    block = scores[b * ROW : (b + 1) * ROW]
    left, right = block[LEFT], block[RIGHT]
    first = lax.broadcasted_iota(jnp.int32, (TILE, 2 * TILE), 1) < TILE
    left = jnp.concatenate([left[: 2 * TILE], jnp.where(first, -jnp.inf, left[2 * TILE :])], axis=0)
    right = jnp.concatenate([jnp.where(first, right[:TILE], -jnp.inf), right[TILE:]], axis=0)
    return left, right


def sides(row):
    return row[:, : 2 * TILE], row[:, 2 * TILE :]


def rows_of(frame, r, count=1):
    return pl.ds(pl.multiple_of((frame * SIDE + r) * ROW, ROW), count * ROW)


def frames_near(frame):
    return jnp.maximum(frame - 1, 0), jnp.minimum(frame + 2, SIDE)


def forward_kernel(
    scale, order_ref, recv_ref, out_ref, grid_ref, log_ref,
    kvq_v, vt_v, weights_v, top_v, total_v, acc_v, in_sem, out_sem,
):
    move_tiles(order_ref, recv_ref, kvq_v, in_sem, True)
    weights_v[...] = jnp.zeros_like(weights_v)
    await_tiles(kvq_v, in_sem)
    transposed(kvq_v.at[1], vt_v)
    factor = scale * LOG2E

    @pl.loop(0, SIDE)
    def _(frame):
        top_v[...] = jnp.full_like(top_v, -jnp.inf)
        total_v[...] = jnp.zeros_like(total_v)
        acc_v[...] = jnp.zeros_like(acc_v)

        @pl.loop(*frames_near(frame))
        def _(other):
            def score(r):
                low, count = window(r)
                return dot(kvq_v[0, rows_of(other, low, count)], kvq_v[2, rows_of(frame, r)], NT)

            def weigh(r, scores):
                low, count = window(r)
                parts = [masked(scores, b) for b in range(count)]
                top = top_v[r : r + 1]
                highest = [
                    functools.reduce(
                        jnp.maximum, [jnp.max(p[side], axis=0, keepdims=True) for p in parts]
                    )
                    for side in range(2)
                ]
                new_top = jnp.maximum(top, jnp.concatenate(highest, axis=1) * factor)
                fade = jnp.exp2(top - new_top)
                tops = sides(new_top)
                sums = [0.0, 0.0]
                for b, p in enumerate(parts):
                    for side, where in enumerate((LEFT, RIGHT)):
                        e = jnp.exp2(p[side] * factor - tops[side])
                        sums[side] += jnp.sum(e, axis=0, keepdims=True)
                        weights_v[(STARTS[r] + b,) + where] = e.astype(BF16)
                total_v[r : r + 1] = total_v[r : r + 1] * fade + jnp.concatenate(sums, axis=1)
                top_v[r : r + 1] = new_top
                weights = weights_v[STARTS[r] : STARTS[r + 1]].reshape(count * ROW, ROW)
                acc_v[r] = acc_v[r] * fade + dot(vt_v[:, rows_of(other, low, count)], weights)

            ahead = score(0)
            for r in range(SIDE):
                scores, ahead = ahead, score(r + 1) if r + 1 < SIDE else None
                weigh(r, scores)

        for r in range(SIDE):
            total = total_v[r : r + 1]
            grid_ref[0, rows_of(frame, r)] = (acc_v[r] / total).T.astype(BF16)
            log_ref[frame, r : r + 1] = top_v[r : r + 1] + jnp.log2(total)

    move_tiles(order_ref, out_ref, grid_ref, out_sem, False)
    await_tiles(grid_ref, out_sem)


def backward_kernel(
    scale, order_ref, recv_ref, grad_ref, att_ref, log_ref, out_ref,
    kvq_v, g_v, out_v, kt_v, dk_acc, dv_acc, weights_v, slopes_v, acc_v, in_sem, grad_sem, out_sem,
):
    head_size = kvq_v.shape[2]
    move_tiles(order_ref, recv_ref, kvq_v, in_sem, True)
    move_tiles(order_ref, grad_ref, g_v, grad_sem, True)
    weights_v[...] = jnp.zeros_like(weights_v)
    slopes_v[...] = jnp.zeros_like(slopes_v)
    dk_acc[...] = jnp.zeros_like(dk_acc)
    dv_acc[...] = jnp.zeros_like(dv_acc)
    await_tiles(kvq_v, in_sem)
    transposed(kvq_v.at[0], kt_v)
    await_tiles(g_v, grad_sem)
    factor = scale * LOG2E
    ones = jnp.ones((8, head_size), BF16)

    @pl.loop(0, SIDE)
    def _(frame):
        acc_v[...] = jnp.zeros_like(acc_v)
        deltas, logs = [], []
        for r in range(SIDE):
            rows = rows_of(frame, r)
            product = g_v[0, rows].astype(F32) * att_ref[0, rows].astype(F32)
            upper = product.astype(BF16)
            lower = (product - upper.astype(F32)).astype(BF16)
            deltas.append(sides((dot(ones, upper, NT) + dot(ones, lower, NT))[:1]))
            logs.append(sides(log_ref[frame, r : r + 1]))

        @pl.loop(*frames_near(frame))
        def _(other):
            def score(r):
                low, count = window(r)
                keys = rows_of(other, low, count)
                rows = rows_of(frame, r)
                return (
                    dot(kvq_v[0, keys], kvq_v[2, rows], NT),
                    dot(kvq_v[1, keys], g_v[0, rows], NT),
                )

            def weigh(r, scores, grad_probs):
                low, count = window(r)
                for b in range(count):
                    parts = masked(scores, b)
                    block = grad_probs[b * ROW : (b + 1) * ROW]
                    for side, where in enumerate((LEFT, RIGHT)):
                        probs = jnp.exp2(parts[side] * factor - logs[r][side])
                        slopes = probs * (block[where] - deltas[r][side])
                        weights_v[(STARTS[r] + b,) + where] = probs.astype(BF16)
                        slopes_v[(STARTS[r] + b,) + where] = slopes.astype(BF16)
                slopes = slopes_v[STARTS[r] : STARTS[r + 1]].reshape(count * ROW, ROW)
                acc_v[r] += dot(kt_v[:, rows_of(other, low, count)], slopes)

            def collect(key_r):
                low, count = window(key_r)
                picks = [STARTS[r] + key_r - window(r)[0] for r in range(low, low + count)]
                keys = rows_of(other, key_r)
                rows = rows_of(frame, low, count)
                dv_acc[keys] += dot(
                    jnp.concatenate([weights_v[b] for b in picks], axis=1), g_v[0, rows]
                )
                dk_acc[keys] += dot(
                    jnp.concatenate([slopes_v[b] for b in picks], axis=1), kvq_v[2, rows]
                )

            ahead = score(0)
            for r in range(SIDE):
                now, ahead = ahead, score(r + 1) if r + 1 < SIDE else None
                weigh(r, *now)
                if r > 0:
                    collect(r - 1)
            collect(SIDE - 1)

        for r in range(SIDE):
            out_v[2, rows_of(frame, r)] = (acc_v[r] * scale).T.astype(BF16)

    out_v[0] = (dk_acc[...] * scale).astype(BF16)
    out_v[1] = dv_acc[...].astype(BF16)
    move_tiles(order_ref, out_ref, out_v, out_sem, False)
    await_tiles(out_v, out_sem)


SMEM = pl.BlockSpec(memory_space=pltpu.SMEM)
ANYWHERE = pl.BlockSpec(memory_space=pl.ANY)
VMEM = pl.BlockSpec(memory_space=pltpu.VMEM)


def attend(order, received):
    shards, _, rows, head_size = received.shape
    tokens = shards * rows
    square = pltpu.VMEM((STARTS[SIDE], ROW, ROW), BF16)
    return pl.pallas_call(
        functools.partial(forward_kernel, head_size**-0.5),
        out_shape=(
            jax.ShapeDtypeStruct((shards, 1, rows, head_size), BF16),
            jax.ShapeDtypeStruct((1, tokens, head_size), BF16),
            jax.ShapeDtypeStruct((SIDE, SIDE, ROW), F32),
        ),
        in_specs=[SMEM, ANYWHERE],
        out_specs=(ANYWHERE, VMEM, VMEM),
        scratch_shapes=[
            pltpu.VMEM((3, tokens, head_size), BF16), pltpu.VMEM((head_size, tokens), BF16), square,
            pltpu.VMEM((SIDE, ROW), F32), pltpu.VMEM((SIDE, ROW), F32),
            pltpu.VMEM((SIDE, head_size, ROW), F32),
            pltpu.SemaphoreType.DMA, pltpu.SemaphoreType.DMA,
        ],
        compiler_params=pltpu.CompilerParams(vmem_limit_bytes=36 * 1024 * 1024),
        cost_estimate=pl.CostEstimate(
            flops=8 * 10**9, bytes_accessed=4 * tokens * head_size * 2, transcendentals=6 * 10**6
        ),
        name="attend",
    )(order, received)


def attend_back(order, received, grad, attended, log_total):
    shards, _, rows, head_size = received.shape
    tokens = shards * rows
    square = pltpu.VMEM((STARTS[SIDE], ROW, ROW), BF16)
    total = pltpu.VMEM((tokens, head_size), F32)
    return pl.pallas_call(
        functools.partial(backward_kernel, head_size**-0.5),
        out_shape=jax.ShapeDtypeStruct((shards, 3, rows, head_size), BF16),
        in_specs=[SMEM, ANYWHERE, ANYWHERE, VMEM, VMEM],
        out_specs=ANYWHERE,
        scratch_shapes=[
            pltpu.VMEM((3, tokens, head_size), BF16), pltpu.VMEM((1, tokens, head_size), BF16),
            pltpu.VMEM((3, tokens, head_size), BF16),
            pltpu.VMEM((head_size, tokens), BF16), total, total, square, square,
            pltpu.VMEM((SIDE, head_size, ROW), F32),
            pltpu.SemaphoreType.DMA, pltpu.SemaphoreType.DMA, pltpu.SemaphoreType.DMA,
        ],
        compiler_params=pltpu.CompilerParams(vmem_limit_bytes=36 * 1024 * 1024),
        cost_estimate=pl.CostEstimate(
            flops=18 * 10**9, bytes_accessed=8 * tokens * head_size * 2, transcendentals=6 * 10**6
        ),
        name="attend_back",
    )(order, received, grad, attended, log_total)


def place_weight(coords_ref, near, far, weight_v, sem):
    width = near[0].shape[2]
    for other, pieces in enumerate((near, far)):
        for dy, piece in enumerate(pieces):
            column = pl.multiple_of(lax.rem(coords_ref[0] + dy, SIDE) * width, 128)
            half = jnp.bitwise_xor(coords_ref[1], other)
            pltpu.make_async_copy(
                piece, weight_v.at[:, half, :, pl.ds(column, width)], sem
            ).start()


def project_back_kernel(coords_ref, cot_ref, *refs):
    near, far = refs[:SIDE], refs[SIDE : 2 * SIDE]
    first_ref, out_ref, weight_v, sem = refs[2 * SIDE :]
    place_weight(coords_ref, near, far, weight_v, sem)
    pltpu.make_async_copy(weight_v, weight_v, sem).wait()
    heads = out_ref.shape[0] // 2
    rows, size = out_ref.shape[2:]
    for pair in range(heads // 2):
        grads = dot(
            cot_ref[...], weight_v[4 * pair : 4 * pair + 4].reshape(2 * size, -1), NT
        ).astype(BF16)
        for video in range(2):
            for one in range(2):
                out_ref[video * heads + pair * 2 + one, 0] = grads[
                    video * rows : (video + 1) * rows, one * size : (one + 1) * size
                ]


def weight_grad_kernel(coords_ref, att_ref, cot_ref, first_ref, keep_ref, send_ref):
    y, core = coords_ref[0], coords_ref[1]
    heads = att_ref.shape[0] // 2
    width = keep_ref.shape[2]
    cot = cot_ref[...]
    mine = jnp.broadcast_to(core == 0, (TILE, cot.shape[1]))
    for head in range(heads):
        both = jnp.concatenate([att_ref[head, 0], att_ref[heads + head, 0]], axis=0)
        part = lax.dot_general(both, cot, (((0,), (0,)), ((), ())), preferred_element_type=F32)
        keep = jnp.where(mine, part[:TILE], part[TILE:]).astype(BF16)
        send = jnp.where(mine, part[TILE:], part[:TILE]).astype(BF16)
        line = slice(head * TILE, (head + 1) * TILE)
        for block in range(SIDE):
            dy = lax.rem(block - y + SIDE, SIDE)
            columns = slice(block * width, (block + 1) * width)
            keep_ref[dy, line] = keep[:, columns]
            send_ref[dy, line] = send[:, columns]


def output_kernel(coords_ref, att_ref, *refs):
    near, far = refs[:SIDE], refs[SIDE : 2 * SIDE]
    first_ref, out_ref, weight_v, att_v, sem = refs[2 * SIDE :]
    place_weight(coords_ref, near, far, weight_v, sem)
    heads = att_ref.shape[0] // 2
    rows, size = att_ref.shape[2:]
    for head in range(heads):
        for video in range(2):
            att_v[video * rows : (video + 1) * rows, head * size : (head + 1) * size] = att_ref[
                video * heads + head, 0
            ]
    pltpu.make_async_copy(weight_v, weight_v, sem).wait()
    weight = weight_v[...].reshape(att_v.shape[1], -1)
    out_ref[...] = dot(att_v[...], weight).astype(BF16)


def project_back(coords, cot_rows, near, far, heads, size, first):
    rows, columns = cot_rows.shape
    units = 2 * heads
    return pl.pallas_call(
        project_back_kernel,
        out_shape=jax.ShapeDtypeStruct((2 * heads, 1, rows // 2, size), BF16),
        in_specs=[SMEM, VMEM] + [ANYWHERE] * (2 * SIDE + 1),
        out_specs=VMEM,
        scratch_shapes=[pltpu.VMEM((units, 2, TILE // 2, columns), BF16), pltpu.SemaphoreType.DMA],
        compiler_params=pltpu.CompilerParams(vmem_limit_bytes=VMEM_BYTES),
        cost_estimate=pl.CostEstimate(
            flops=2 * rows * columns * heads * size, bytes_accessed=9 * 10**6, transcendentals=0
        ),
        name="project_back",
    )(coords, cot_rows, *near, *far, first)


def weight_grad_parts(coords, attended, cot_rows, width, first):
    units, _, _, size = attended.shape
    rows, columns = cot_rows.shape
    half = jax.ShapeDtypeStruct((SIDE, units * size // 4, width), BF16)
    return pl.pallas_call(
        weight_grad_kernel,
        out_shape=(half, half),
        in_specs=[SMEM, VMEM, VMEM, ANYWHERE],
        out_specs=(VMEM, VMEM),
        compiler_params=pltpu.CompilerParams(vmem_limit_bytes=40 * 1024 * 1024),
        cost_estimate=pl.CostEstimate(
            flops=rows * columns * units * size, bytes_accessed=8 * 10**6, transcendentals=0
        ),
        name="weight_grad_parts",
    )(coords, attended, cot_rows, first)


def project(coords, attended, columns, near, far, first):
    units, _, depth, size = attended.shape
    rows, heads = 2 * depth, units // 2
    return pl.pallas_call(
        output_kernel,
        out_shape=jax.ShapeDtypeStruct((rows, columns), BF16),
        in_specs=[SMEM, VMEM] + [ANYWHERE] * (2 * SIDE + 1),
        out_specs=VMEM,
        scratch_shapes=[
            pltpu.VMEM((units, 2, TILE // 2, columns), BF16), pltpu.VMEM((rows, heads * size), BF16),
            pltpu.SemaphoreType.DMA,
        ],
        compiler_params=pltpu.CompilerParams(vmem_limit_bytes=40 * 1024 * 1024),
        cost_estimate=pl.CostEstimate(
            flops=2 * rows * columns * heads * size, bytes_accessed=8 * 10**6, transcendentals=0
        ),
        name="project",
    )(coords, attended, *near, *far, first)


def along_y(array, step):
    return lax.ppermute(array, "dp", [(i, (i + step) % SIDE) for i in range(SIDE)])


def to_other_core(array):
    return lax.ppermute(array, "seq", [(i, i ^ 1) for i in range(lax.axis_size("seq"))])


def summed(terms):
    return functools.reduce(jnp.add, [t.astype(F32) for t in terms])


def scatter_near(keep, send):
    total = summed([keep, to_other_core(send)]).astype(BF16)
    return summed([total[0]] + [along_y(total[d], d) for d in range(1, SIDE)]).astype(BF16)


def scatter_far(total):
    shards = lax.axis_size("seq")
    total = lax.all_to_all(
        total.reshape(shards // 2, TILE, -1), "seq", split_axis=0, concat_axis=0, tiled=True,
        axis_index_groups=[list(range(core, shards, 2)) for core in range(2)],
    )
    return jnp.sum(total.astype(F32), axis=0)


def gather_weight(block):
    shards = lax.axis_size("seq")
    depth, width = block.shape
    sent = jnp.broadcast_to(
        block.reshape(1, 2, depth // 2, width), (shards // 2, 2, depth // 2, width)
    )
    return exchange(sent.reshape(shards, depth // 2, width))


def pack_kernel(*refs):
    out_ref = refs[-1]
    for index, ref in enumerate(refs[:-1]):
        out_ref[:, index] = jnp.swapaxes(ref[...], 0, 1)


def pack(arrays):
    tokens, units, size = arrays[0].shape
    step = tokens // 4
    return pl.pallas_call(
        pack_kernel,
        grid=(4,),
        out_shape=jax.ShapeDtypeStruct((units, len(arrays), tokens, size), BF16),
        in_specs=[pl.BlockSpec((step, units, size), lambda i: (i, 0, 0))] * len(arrays),
        out_specs=pl.BlockSpec((units, len(arrays), step, size), lambda i: (0, 0, i, 0)),
        compiler_params=pltpu.CompilerParams(vmem_limit_bytes=VMEM_BYTES),
        name="pack",
    )(*arrays)


def unpack_kernel(in_ref, *refs):
    for index, ref in enumerate(refs):
        ref[...] = jnp.swapaxes(in_ref[:, index], 0, 1)


def unpack(array):
    units, count, tokens, size = array.shape
    step = tokens // 4
    return pl.pallas_call(
        unpack_kernel,
        grid=(4,),
        out_shape=[jax.ShapeDtypeStruct((tokens, units, size), BF16)] * count,
        in_specs=[pl.BlockSpec((units, count, step, size), lambda i: (0, 0, i, 0))],
        out_specs=[pl.BlockSpec((step, units, size), lambda i: (i, 0, 0))] * count,
        compiler_params=pltpu.CompilerParams(vmem_limit_bytes=40 * 1024 * 1024),
        name="unpack",
    )(array)


def after_kernel(array_ref, *refs):
    pass


def after(array, *first):
    return pl.pallas_call(
        after_kernel,
        out_shape=jax.ShapeDtypeStruct(array.shape, array.dtype),
        in_specs=[ANYWHERE] * (1 + len(first)),
        out_specs=ANYWHERE,
        input_output_aliases={0: 0},
        name="after",
    )(array, *first)


def exchange(array):
    return lax.all_to_all(array, "seq", split_axis=0, concat_axis=0, tiled=True)


def local(queries, keys_in, values_in, pair_keys, out_weight, cotangent):
    rows, videos, heads, head_size = queries.shape
    columns = cotangent.shape[2]
    coords = jnp.stack([lax.axis_index("dp"), lax.axis_index("seq") % 2]).astype(jnp.int32)
    units = videos * heads
    order = grid_order(pair_keys)
    cot_rows = jnp.transpose(cotangent, (1, 0, 2)).reshape(videos * rows, columns)
    packed = pack([a.reshape(rows, units, head_size) for a in (keys_in, values_in, queries)])
    block = gather_weight(out_weight)
    received = exchange(after(packed, block, order, cot_rows))
    near = [block] + [along_y(block, -d) for d in range(1, SIDE)]
    far = [to_other_core(piece) for piece in near]
    grad_sent = project_back(coords, cot_rows, near, far, heads, head_size, order)
    grad_received = exchange(grad_sent)
    received = after(received, grad_sent)
    attended, attended_grid, log_total = attend(order, received)
    attended_tok = exchange(attended)
    grads_sent = attend_back(order, received, grad_received, attended_grid, log_total)
    total = scatter_near(
        *weight_grad_parts(coords, attended_tok, cot_rows, out_weight.shape[1], grads_sent)
    )
    output = project(coords, attended_tok, columns, near, far, total)
    output = jnp.transpose(output.reshape(videos, rows, columns), (1, 0, 2))
    grad_k, grad_v, grad_q = (a.reshape(queries.shape) for a in unpack(exchange(grads_sent)))
    return output, grad_q, grad_k, grad_v, scatter_far(total)


def solution(mesh):
    placed = (
        P("seq", "dp", None, None),
        P("seq", "dp", None, None),
        P("seq", "dp", None, None),
        P(),
        P("seq", "dp"),
        P("seq", "dp", None),
    )
    return jax.shard_map(
        local,
        mesh=mesh,
        in_specs=placed,
        out_specs=(
            P("seq", "dp", None),
            P("seq", "dp", None, None),
            P("seq", "dp", None, None),
            P("seq", "dp", None, None),
            P("seq", "dp"),
        ),
        check_vma=False,
    )
```

time: 918 us -> 236 us (0.26)
  matrix products: 505 us -> 0 us
  local copies, waits for them, and re-layouts: 169 us -> 20.2 us
  Pallas kernels: 0 us -> 72.9 us
  loops' own time: 31.7 us -> 0 us
  other arithmetic: 36.2 us -> 8.76 us
  waiting for transfers between devices: 101 us -> 80.2 us
  blocking collectives: 13.5 us -> 0 us
  between operations: 14.3 us -> 0.85 us
  starting transfers between devices: 39.4 us -> 51.6 us
    dot_general x83 -> x0, matrix products: 505 us -> none  [the longest x8 136 us: one_block(): jnp.einsum('qatb,qad->tbd', scores_dense, query_block, preferred_element_...]
    ppermute x0 -> x11, waiting for transfers between devices: none -> 74 us  [the longest x6 72 us: along_y(): lax.ppermute(array, 'dp', [(i, (i + step) % SIDE) for i in range(SIDE)])]
    pallas_call x0 -> x10, Pallas kernels: none -> 72.9 us  [the longest x1 26.4 us: attend_back(): pl.pallas_call(functools.partial(backward_kernel, head_size ** (-0.5)), o...]
    all_to_all x8 -> x6, waiting for transfers between devices: 77.5 us -> 6.22 us  [the longest x1 3.8 us: scatter_far(): lax.all_to_all(total.reshape(shards // 2, TILE, -1), 'seq', split_axis=0,...]
    dynamic_update_slice x8 -> x0, local copies, waits for them, and re-layouts: 59.7 us -> none  [unit_forward(): lax.map(one_block, (query_blocks, key_table))]
    another operation x2 -> x0, loops' own time: 31.7 us -> none  [the longest x1 30.7 us: unit_backward(): lax.scan(one_block, (empty_acc, empty_acc), packed)]
    squeeze x8 -> x1, local copies, waits for them, and re-layouts: 29.5 us -> 0.24 us  [scatter_near(): total[d]]
    unnamed x4 -> x0, waiting for transfers between devices: 23.7 us -> none
  transfers between devices with their start and end apart: 11 -> 17, of which waited for: 8 -> 7; matrix products, arithmetic and copies ran while one was open for 75% -> 5% of each run, Pallas kernels for 0% -> 29%
where the time goes in v1:
time: 236 us; the launch traced here: 234 us
  waiting for transfers between devices  80.2 us (34%)
  Pallas kernels  72.9 us (31%)
  starting transfers between devices  51.6 us (22%)
  local copies, waits for them, and re-layouts  20.2 us (9%)
  other arithmetic  8.76 us (4%)
    ppermute x6, waiting for transfers between devices, along_y(): lax.ppermute(array, 'dp', [(i, (i + step) % SIDE) for i in range(SIDE)])  72 us
    all_to_all x5, starting transfers between devices, exchange(): return lax.all_to_all(array, 'seq', split_axis=0, concat_axis=0, tiled=True)  35.5 us
    pallas_call x1, Pallas kernels, attend_back(): pl.pallas_call(functools.partial(backward_kernel, head_size ** (-0.5)), o...  26.4 us
    pallas_call x1, Pallas kernels, attend(): pl.pallas_call(functools.partial(forward_kernel, head_size ** (-0.5)), ou...  19.6 us
    unnamed x31, local copies, waits for them, and re-layouts  14.3 us
    ppermute x6, starting transfers between devices, along_y(): lax.ppermute(array, 'dp', [(i, (i + step) % SIDE) for i in range(SIDE)])  8.54 us
    all_to_all x1, starting transfers between devices, scatter_far(): lax.all_to_all(total.reshape(shards // 2, TILE, -1), 'seq', split_axis=0,...  7.02 us
    pallas_call x1, Pallas kernels, project_back(): pl.pallas_call(project_back_kernel, out_shape=jax.ShapeDtypeStruct((2 * h...  6.75 us
  transfers between devices with their start and end apart: 17, of which 7 were waited for; matrix products, arithmetic and copies ran while one was open for 5% of the time, Pallas kernels for 29%

profile of v1, /device:TPU:0, one launch (start us, length us, event | category | flops | bytes accessed | tf_op | source)
XLA Modules:
  0.0 234.5 jit_solution(5381393615267953146)
XLA Ops:
  2.4 8.2 %all-to-all-start = ((bf16[32,32,384]{2,1,0:T(8,128)(2,1)}), bf16[32,32,384]{2,1,0:T(8,128)(2,1)S(1)}, u32[]{:S(2)}, u32[]{:S(2)}) async-start(bf16[32,32,384]{2,1,0:T(8,128)(2,1)} %bitcast.6), calls=%async_computation | async-start | bytes 1572864 | tf_op jit(solution)/shard_map/all_to_all | solution.py:526
  12.1 2.6 %grid_order.1 = s32[64,1]{1,0:T(8,128)} custom-call(s32[64,27]{1,0:T(8,128)} %copy.16.pairs_ref), custom_call_target="tpu_custom_call" | custom-call | tf_op jit(solution)/shard_map/grid_order/pallas_call | solution.py:61
  14.7 2.1 copy.17
  18.2 4.6 %pack.1.array_ref = bf16[32,3,128,128]{3,2,1,0:T(8,128)(2,1)} custom-call(bf16[128,32,128]{2,1,0:T(8,128)(2,1)} %bitcast.33, bf16[128,32,128]{2,1,0:T(8,128)(2,1)} %bitcast.34, bf16[128,32,128]{2,1,0:T(8,128)(2,1)} %bitcast.35), custom_call_target="tpu_custom_call" | custom-call | tf_op jit(solution)/shard_map/pack/pallas_call | solution.py:480
  22.8 2.4 %all-to-all-done.refs_0_ = bf16[32,32,384]{2,1,0:T(8,128)(2,1)S(1)} async-done(((bf16[32,32,384]{2,1,0:T(8,128)(2,1)}), bf16[32,32,384]{2,1,0:T(8,128)(2,1)S(1)}, u32[]{:S(2)}, u32[]{:S(2)}) %all-to-all-start) | async-done | bytes 786464 | tf_op jit(solution)/shard_map/all_to_all | solution.py:526
  26.1 5.0 %all-to-all-start.1 = ((bf16[32,3,128,128]{3,2,1,0:T(8,128)(2,1)}), bf16[32,3,128,128]{3,2,1,0:T(8,128)(2,1)S(1)}, u32[]{:S(2)}, u32[]{:S(2)}) async-start(bf16[32,3,128,128]{3,2,1,0:T(8,128)(2,1)} %after.2), calls=%async_computation.1 | async-start | bytes 6291456 | tf_op jit(solution)/shard_map/all_to_all | solution.py:526
  31.1 3.1 %collective-permute-start = (bf16[32,32,384]{2,1,0:T(8,128)(2,1)}, bf16[32,32,384]{2,1,0:T(8,128)(2,1)}, u32[]{:S(2)}, u32[]{:S(2)}) collective-permute-start(bf16[32,32,384]{2,1,0:T(8,128)(2,1)} %copy-done.3), channel_id=1, source_target_pairs={{0,96},{32,0},{64,32},{96,64},{1,97},{33,1},{65,33},{97,65},{2,98}... | collective-permute-start | bytes 2359304 | tf_op jit(solution)/shard_map/ppermute | solution.py:437
  35.8 32.8 %collective-permute-done.refs_1_ = bf16[32,32,384]{2,1,0:T(8,128)(2,1)} collective-permute-done((bf16[32,32,384]{2,1,0:T(8,128)(2,1)}, bf16[32,32,384]{2,1,0:T(8,128)(2,1)}, u32[]{:S(2)}, u32[]{:S(2)}) %collective-permute-start) | collective-permute-done | bytes 786464 | tf_op jit(solution)/shard_map/ppermute | solution.py:437
  69.1 3.2 %collective-permute-done.2.refs_3_ = bf16[32,32,384]{2,1,0:T(8,128)(2,1)} collective-permute-done((bf16[32,32,384]{2,1,0:T(8,128)(2,1)}, bf16[32,32,384]{2,1,0:T(8,128)(2,1)}, u32[]{:S(2)}, u32[]{:S(2)}) %collective-permute-start.2) | collective-permute-done | bytes 786464 | tf_op jit(solution)/shard_map/ppermute | solution.py:437
  74.9 6.8 %project_back.1.refs_0_ = bf16[32,1,128,128]{3,2,1,0:T(8,128)(2,1)} custom-call(s32[2]{0:T(128)} %pad_add_fusion.coords_ref, bf16[256,1536]{1,0:T(8,128)(2,1)} %bitcast.30, bf16[32,32,384]{2,1,0:T(8,128)(2,1)} %copy-done.3, bf16[32,32,384]{2,1,0:T(8,128)(2,1)} %collective-permute-done.refs_1_, bf16[32,32,384]{2,1,0:T(8,128)(2,1)} %collective-permute-done.1.refs_2_, ...), custom_call_target="tpu_custom_call" | custom-call | flops 1610612736 | bytes 9000000 | tf_op jit(solution)/shard_map/project_back/pallas_call | solution.py:385
  81.7 7.4 %all-to-all-start.3 = ((bf16[32,1,128,128]{3,2,1,0:T(8,128)(2,1)}), bf16[32,1,128,128]{3,2,1,0:T(8,128)(2,1)}, u32[]{:S(2)}, u32[]{:S(2)}) async-start(bf16[32,1,128,128]{3,2,1,0:T(8,128)(2,1)} %project_back.1.refs_0_), calls=%async_computation.3 | async-start | bytes 2097152 | tf_op jit(solution)/shard_map/all_to_all | solution.py:526
  91.7 19.6 %attend.1 = (bf16[32,1,128,128]{3,2,1,0:T(8,128)(2,1)S(1)}, bf16[1,4096,128]{2,1,0:T(8,128)(2,1)S(1)}, f32[4,4,256]{2,1,0:T(4,128)S(1)}) custom-call(s32[64]{0:T(128)S(1)} %copy-done.11, bf16[32,3,128,128]{3,2,1,0:T(8,128)(2,1)S(1)} %copy-done.1), custom_call_target="tpu_custom_call" | custom-call | flops 8000000000 | bytes 4194304 | tf_op jit(solution)/shard_map/attend/pallas_call | solution.py:270
  113.2 7.6 %all-to-all-start.2 = ((bf16[32,1,128,128]{3,2,1,0:T(8,128)(2,1)}), bf16[32,1,128,128]{3,2,1,0:T(8,128)(2,1)}, u32[]{:S(2)}, u32[]{:S(2)}) async-start(bf16[32,1,128,128]{3,2,1,0:T(8,128)(2,1)} %copy-done.10), calls=%async_computation.2 | async-start | bytes 2097152 | tf_op jit(solution)/shard_map/all_to_all | solution.py:526
  122.1 26.4 %attend_back.1.first_ref = bf16[32,3,128,128]{3,2,1,0:T(8,128)(2,1)S(1)} custom-call(s32[64]{0:T(128)S(1)} %copy-done.11, bf16[32,3,128,128]{3,2,1,0:T(8,128)(2,1)S(1)} %copy-done.2, bf16[32,1,128,128]{3,2,1,0:T(8,128)(2,1)} %all-to-all-done.3.grad_ref, bf16[1,4096,128]{2,1,0:T(8,128)(2,1)S(1)} %copy-done.14, f32[4,4,256]{2,1,0:T(4,128)S(1)} %get-tuple-element.15.log_ref), custom_call_target="tpu_custom_call" | custom-call | flops 17999998976 | bytes 8388608 | tf_op jit(solution)/shard_map/attend_back/pallas_call | solution.py:298
  153.1 4.8 %weight_grad_parts.1 = (bf16[4,1024,384]{2,1,0:T(8,128)(2,1)S(1)}, bf16[4,1024,384]{2,1,0:T(8,128)(2,1)}) custom-call(s32[2]{0:T(128)S(1)} %copy-done.12, bf16[32,1,128,128]{3,2,1,0:T(8,128)(2,1)} %all-to-all-done.2.att_ref, bf16[256,1536]{1,0:T(8,128)(2,1)S(1)} %bitcast.31, bf16[32,3,128,128]{3,2,1,0:T(8,128)(2,1)S(1)} %copy-done.8), custom_call_target="tpu_custom_call" | custom-call | flops 1610612736 | bytes 8000000 | tf_op jit(solution)/shard_map/weight_grad_parts/pallas_call | solution.py:403
  159.7 7.3 %all-to-all-start.4 = ((bf16[32,3,128,128]{3,2,1,0:T(8,128)(2,1)}), bf16[32,3,128,128]{3,2,1,0:T(8,128)(2,1)S(1)}, u32[]{:S(2)}, u32[]{:S(2)}) async-start(bf16[32,3,128,128]{3,2,1,0:T(8,128)(2,1)} %copy-done.7), calls=%async_computation.4 | async-start | bytes 6291456 | tf_op jit(solution)/shard_map/all_to_all | solution.py:526
  167.0 3.6 %add_convert_fusion = bf16[4,1024,384]{2,1,0:T(8,128)(2,1)S(1)} fusion(bf16[4,1024,384]{2,1,0:T(8,128)(2,1)} %collective-permute-done.7, bf16[4,1024,384]{2,1,0:T(8,128)(2,1)} %copy-done.9), kind=kLoop, calls=%fused_computation | loop fusion | flops 6291456 | bytes 9437184 | tf_op jit(solution)/shard_map/convert_element_type | solution.py:449
  170.8 2.3 collective-permute-start.10
  174.7 32.6 %collective-permute-done.10 = bf16[1024,384]{1,0:T(8,128)(2,1)S(1)} collective-permute-done((bf16[1024,384]{1,0:T(8,128)(2,1)S(1)}, bf16[1024,384]{1,0:T(8,128)(2,1)S(1)}, u32[]{:S(2)}, u32[]{:S(2)}) %collective-permute-start.10) | collective-permute-done | bytes 786464 | tf_op jit(solution)/shard_map/ppermute | solution.py:437
  207.3 3.4 %collective-permute-done.8 = bf16[1024,384]{1,0:T(8,128)(2,1)S(1)} collective-permute-done((bf16[1024,384]{1,0:T(8,128)(2,1)S(1)}, bf16[1024,384]{1,0:T(8,128)(2,1)S(1)}, u32[]{:S(2)}, u32[]{:S(2)}) %collective-permute-start.8) | collective-permute-done | bytes 786464 | tf_op jit(solution)/shard_map/ppermute | solution.py:437
  211.9 7.0 %all-to-all-start.5 = ((bf16[16,64,384]{2,1,0:T(8,128)(2,1)}), bf16[16,64,384]{2,1,0:T(8,128)(2,1)}, u32[]{:S(2)}, u32[]{:S(2)}) async-start(bf16[16,64,384]{2,1,0:T(8,128)(2,1)} %bitcast.28), calls=%async_computation.5 | async-start | bytes 1572864 | tf_op jit(solution)/shard_map/all_to_all | solution.py:455
  219.0 2.4 %unpack.1 = (bf16[128,32,128]{2,1,0:T(8,128)(2,1)}, bf16[128,32,128]{2,1,0:T(8,128)(2,1)}, bf16[128,32,128]{2,1,0:T(8,128)(2,1)}) custom-call(bf16[32,3,128,128]{3,2,1,0:T(8,128)(2,1)S(1)} %all-to-all-done.4.in_ref), custom_call_target="tpu_custom_call" | custom-call | tf_op jit(solution)/shard_map/unpack/pallas_call | solution.py:499
  221.4 5.7 %project.1 = bf16[256,1536]{1,0:T(8,128)(2,1)S(1)} custom-call(s32[2]{0:T(128)S(1)} %copy-done.12, bf16[32,1,128,128]{3,2,1,0:T(8,128)(2,1)} %all-to-all-done.2.att_ref, bf16[32,32,384]{2,1,0:T(8,128)(2,1)S(1)} %copy-done.4, bf16[32,32,384]{2,1,0:T(8,128)(2,1)} %collective-permute-done.refs_1_, bf16[32,32,384]{2,1,0:T(8,128)(2,1)} %collective-permute-done.1.refs_2_, ...), custom_call_target="tpu_custom_call" | custom-call | flops 1610612736 | bytes 8000000 | tf_op jit(solution)/shard_map/project/pallas_call | solution.py:419
  228.8 3.8 %all-to-all-done.5 = bf16[16,64,384]{2,1,0:T(8,128)(2,1)} async-done(((bf16[16,64,384]{2,1,0:T(8,128)(2,1)}), bf16[16,64,384]{2,1,0:T(8,128)(2,1)}, u32[]{:S(2)}, u32[]{:S(2)}) %all-to-all-start.5) | async-done | bytes 786464 | tf_op jit(solution)/shard_map/all_to_all | solution.py:455
  (60 shorter events, 28.9 us)
Async XLA Ops:
  2.4 22.8 %all-to-all-start = ((bf16[32,32,384]{2,1,0:T(8,128)(2,1)}), bf16[32,32,384]{2,1,0:T(8,128)(2,1)S(1)}, u32[]{:S(2)}, u32[]{:S(2)}) async-start(bf16[32,32,384]{2,1,0:T(8,128)(2,1)} %bitcast.6), calls=%async_computation | async-start | bytes 1572864 | tf_op jit(solution)/shard_map/all_to_all | solution.py:526
  26.1 55.6 %all-to-all-start.1 = ((bf16[32,3,128,128]{3,2,1,0:T(8,128)(2,1)}), bf16[32,3,128,128]{3,2,1,0:T(8,128)(2,1)S(1)}, u32[]{:S(2)}, u32[]{:S(2)}) async-start(bf16[32,3,128,128]{3,2,1,0:T(8,128)(2,1)} %after.2), calls=%async_computation.1 | async-start | bytes 6291456 | tf_op jit(solution)/shard_map/all_to_all | solution.py:526
  31.1 37.5 %collective-permute-start = (bf16[32,32,384]{2,1,0:T(8,128)(2,1)}, bf16[32,32,384]{2,1,0:T(8,128)(2,1)}, u32[]{:S(2)}, u32[]{:S(2)}) collective-permute-start(bf16[32,32,384]{2,1,0:T(8,128)(2,1)} %copy-done.3), channel_id=1, source_target_pairs={{0,96},{32,0},{64,32},{96,64},{1,97},{33,1},{65,33},{97,65},{2,98}... | collective-permute-start | bytes 2359304 | tf_op jit(solution)/shard_map/ppermute | solution.py:437
  34.2 34.4 %collective-permute-start.1 = (bf16[32,32,384]{2,1,0:T(8,128)(2,1)}, bf16[32,32,384]{2,1,0:T(8,128)(2,1)}, u32[]{:S(2)}, u32[]{:S(2)}) collective-permute-start(bf16[32,32,384]{2,1,0:T(8,128)(2,1)} %copy-done.3), channel_id=1, source_target_pairs={{0,64},{32,96},{64,0},{96,32},{1,65},{33,97},{65,1},{97,33},{2,66}... | collective-permute-start | bytes 2359304 | tf_op jit(solution)/shard_map/ppermute | solution.py:437
  34.8 37.5 %collective-permute-start.2 = (bf16[32,32,384]{2,1,0:T(8,128)(2,1)}, bf16[32,32,384]{2,1,0:T(8,128)(2,1)}, u32[]{:S(2)}, u32[]{:S(2)}) collective-permute-start(bf16[32,32,384]{2,1,0:T(8,128)(2,1)} %copy-done.3), channel_id=1, source_target_pairs={{0,32},{32,64},{64,96},{96,0},{1,33},{33,65},{65,97},{97,1},{2,34}... | collective-permute-start | bytes 2359304 | tf_op jit(solution)/shard_map/ppermute | solution.py:437
  35.8 37.1 %collective-permute-start.3 = (bf16[32,32,384]{2,1,0:T(8,128)(2,1)}, bf16[32,32,384]{2,1,0:T(8,128)(2,1)}, u32[]{:S(2)}, u32[]{:S(2)}) collective-permute-start(bf16[32,32,384]{2,1,0:T(8,128)(2,1)} %copy-done.3), channel_id=1, source_target_pairs={{0,1},{1,0},{2,3},{3,2},{4,5},{5,4},{6,7},{7,6},{8,9},{9,8},{10,11... | collective-permute-start | bytes 2359304 | tf_op jit(solution)/shard_map/ppermute | solution.py:441
  68.6 4.3 %collective-permute-start.4 = (bf16[32,32,384]{2,1,0:T(8,128)(2,1)}, bf16[32,32,384]{2,1,0:T(8,128)(2,1)}, u32[]{:S(2)}, u32[]{:S(2)}) collective-permute-start(bf16[32,32,384]{2,1,0:T(8,128)(2,1)} %collective-permute-done.refs_1_), channel_id=1, source_target_pairs={{0,1},{1,0},{2,3},{3,2},{4,5},{5,4},{6,7},{7,6},{8,9},{9,8},{10,11... | collective-permute-start | bytes 2359304 | tf_op jit(solution)/shard_map/ppermute | solution.py:441
  68.6 4.3 %collective-permute-start.5 = (bf16[32,32,384]{2,1,0:T(8,128)(2,1)}, bf16[32,32,384]{2,1,0:T(8,128)(2,1)}, u32[]{:S(2)}, u32[]{:S(2)}) collective-permute-start(bf16[32,32,384]{2,1,0:T(8,128)(2,1)} %collective-permute-done.1.refs_2_), channel_id=1, source_target_pairs={{0,1},{1,0},{2,3},{3,2},{4,5},{5,4},{6,7},{7,6},{8,9},{9,8},{10,11... | collective-permute-start | bytes 2359304 | tf_op jit(solution)/shard_map/ppermute | solution.py:441
  72.3 2.6 %collective-permute-start.6 = (bf16[32,32,384]{2,1,0:T(8,128)(2,1)}, bf16[32,32,384]{2,1,0:T(8,128)(2,1)}, u32[]{:S(2)}, u32[]{:S(2)}) collective-permute-start(bf16[32,32,384]{2,1,0:T(8,128)(2,1)} %collective-permute-done.2.refs_3_), channel_id=1, source_target_pairs={{0,1},{1,0},{2,3},{3,2},{4,5},{5,4},{6,7},{7,6},{8,9},{9,8},{10,11... | collective-permute-start | bytes 2359304 | tf_op jit(solution)/shard_map/ppermute | solution.py:441
  81.7 7.4 %copy-start = (bf16[32,3,128,128]{3,2,1,0:T(8,128)(2,1)}, bf16[32,3,128,128]{3,2,1,0:T(8,128)(2,1)S(1)}, u32[]{:S(2)}) copy-start(bf16[32,3,128,128]{3,2,1,0:T(8,128)(2,1)S(1)} %all-to-all-done.1.array_ref) | copy-start | bytes 9437188
  81.7 31.5 %all-to-all-start.3 = ((bf16[32,1,128,128]{3,2,1,0:T(8,128)(2,1)}), bf16[32,1,128,128]{3,2,1,0:T(8,128)(2,1)}, u32[]{:S(2)}, u32[]{:S(2)}) async-start(bf16[32,1,128,128]{3,2,1,0:T(8,128)(2,1)} %project_back.1.refs_0_), calls=%async_computation.3 | async-start | bytes 2097152 | tf_op jit(solution)/shard_map/all_to_all | solution.py:526
  89.8 1.9 copy-start.1
  91.7 29.2 %copy-start.2 = (bf16[32,3,128,128]{3,2,1,0:T(8,128)(2,1)S(1)}, bf16[32,3,128,128]{3,2,1,0:T(8,128)(2,1)}, u32[]{:S(2)}) copy-start(bf16[32,3,128,128]{3,2,1,0:T(8,128)(2,1)} %after.3.recv_ref) | copy-start | bytes 9437188
  113.2 36.9 %all-to-all-start.2 = ((bf16[32,1,128,128]{3,2,1,0:T(8,128)(2,1)}), bf16[32,1,128,128]{3,2,1,0:T(8,128)(2,1)}, u32[]{:S(2)}, u32[]{:S(2)}) async-start(bf16[32,1,128,128]{3,2,1,0:T(8,128)(2,1)} %copy-done.10), calls=%async_computation.2 | async-start | bytes 2097152 | tf_op jit(solution)/shard_map/all_to_all | solution.py:526
  122.1 28.1 %copy-start.12 = (s32[2]{0:T(128)S(1)}, s32[2]{0:T(128)}, u32[]{:S(2)}) copy-start(s32[2]{0:T(128)} %pad_add_fusion.coords_ref) | copy-start | bytes 28
  151.2 1.9 copy-start.8
  159.7 7.3 %collective-permute-start.7 = (bf16[4,1024,384]{2,1,0:T(8,128)(2,1)}, bf16[4,1024,384]{2,1,0:T(8,128)(2,1)}, u32[]{:S(2)}, u32[]{:S(2)}) collective-permute-start(bf16[4,1024,384]{2,1,0:T(8,128)(2,1)} %get-tuple-element.17), channel_id=1, source_target_pairs={{0,1},{1,0},{2,3},{3,2},{4,5},{5,4},{6,7},{7,6},{8,9},{9,8},{10,11... | collective-permute-start | bytes 9437192 | tf_op jit(solution)/shard_map/ppermute | solution.py:441
  159.7 52.3 %all-to-all-start.4 = ((bf16[32,3,128,128]{3,2,1,0:T(8,128)(2,1)}), bf16[32,3,128,128]{3,2,1,0:T(8,128)(2,1)S(1)}, u32[]{:S(2)}, u32[]{:S(2)}) async-start(bf16[32,3,128,128]{3,2,1,0:T(8,128)(2,1)} %copy-done.7), calls=%async_computation.4 | async-start | bytes 6291456 | tf_op jit(solution)/shard_map/all_to_all | solution.py:526
  170.8 36.4 %collective-permute-start.10 = (bf16[1024,384]{1,0:T(8,128)(2,1)S(1)}, bf16[1024,384]{1,0:T(8,128)(2,1)S(1)}, u32[]{:S(2)}, u32[]{:S(2)}) collective-permute-start(bf16[1024,384]{1,0:T(8,128)(2,1)S(1)} %get-tuple-element.22), channel_id=1, source_target_pairs={{0,96},{32,0},{64,32},{96,64},{1,97},{33,1},{65,33},{97,65},{2,98}... | collective-permute-start | bytes 2359304 | tf_op jit(solution)/shard_map/ppermute | solution.py:437
  173.1 37.5 %collective-permute-start.8 = (bf16[1024,384]{1,0:T(8,128)(2,1)S(1)}, bf16[1024,384]{1,0:T(8,128)(2,1)S(1)}, u32[]{:S(2)}, u32[]{:S(2)}) collective-permute-start(bf16[1024,384]{1,0:T(8,128)(2,1)S(1)} %get-tuple-element.21), channel_id=1, source_target_pairs={{0,32},{32,64},{64,96},{96,0},{1,33},{33,65},{65,97},{97,1},{2,34}... | collective-permute-start | bytes 2359304 | tf_op jit(solution)/shard_map/ppermute | solution.py:437
  173.1 37.5 %collective-permute-start.9 = (bf16[1024,384]{1,0:T(8,128)(2,1)S(1)}, bf16[1024,384]{1,0:T(8,128)(2,1)S(1)}, u32[]{:S(2)}, u32[]{:S(2)}) collective-permute-start(bf16[1024,384]{1,0:T(8,128)(2,1)S(1)} %get-tuple-element.23), channel_id=1, source_target_pairs={{0,64},{32,96},{64,0},{96,32},{1,65},{33,97},{65,1},{97,33},{2,66}... | collective-permute-start | bytes 2359304 | tf_op jit(solution)/shard_map/ppermute | solution.py:437
  211.9 20.6 %all-to-all-start.5 = ((bf16[16,64,384]{2,1,0:T(8,128)(2,1)}), bf16[16,64,384]{2,1,0:T(8,128)(2,1)}, u32[]{:S(2)}, u32[]{:S(2)}) async-start(bf16[16,64,384]{2,1,0:T(8,128)(2,1)} %bitcast.28), calls=%async_computation.5 | async-start | bytes 1572864 | tf_op jit(solution)/shard_map/all_to_all | solution.py:455
  219.0 2.4 %copy-start.4 = (bf16[32,32,384]{2,1,0:T(8,128)(2,1)S(1)}, bf16[32,32,384]{2,1,0:T(8,128)(2,1)}, u32[]{:S(2)}) copy-start(bf16[32,32,384]{2,1,0:T(8,128)(2,1)} %copy-done.3) | copy-start | bytes 2359300
  219.0 2.4 %copy-start.5 = (bf16[1024,384]{1,0:T(8,128)(2,1)S(1)}, bf16[1024,384]{1,0:T(8,128)(2,1)}, u32[]{:S(2)}) copy-start(bf16[1024,384]{1,0:T(8,128)(2,1)} %fusion.2.refs_8_) | copy-start | bytes 2359300
  (8 other events, 9.2 us)
